TPU v7x, 32 devices: a whole 2x2x4 slice. The times are simulated.
32 devices in a mesh: req: 8 (over z, y), kv: 4 (over x, core).
Axes of the slice: x: 2, y: 2, z: 4, core: 2. Of those that a mesh axis runs over, the one named last changes fastest.
Arguments:
- hidden_in: bfloat16 [8192, 2048], P(('req', 'kv')), may hold values from -6 to 6
- slot_tokens: int32 [8192], replicated, may hold values from 0 to 8191, as said below
- cache_len: int32 [64], P('req'), may hold values from 1 to 2048, 32768 in all
- prefill_start: int32 [8], P('req'), may hold values from 0 to 2048
- key_cache: bfloat16 [64, 2048, 1024], P('req', None, 'kv')
- value_cache: bfloat16 [64, 2048, 1024], P('req', None, 'kv'), may hold values from -18 to 18
- key_prefix: bfloat16 [8, 2048, 1024], P('req', None, 'kv')
- value_prefix: bfloat16 [8, 2048, 1024], P('req', None, 'kv'), may hold values from -18 to 18
- attn_gain: float32 [2048], replicated, may hold values from 0.25 to 1.75
- q_proj: bfloat16 [2048, 2048], P(None, 'kv'), may hold values from -0.125 to 0.125
- k_proj: bfloat16 [2048, 1024], P(None, 'kv'), may hold values from -0.125 to 0.125
- v_proj: bfloat16 [2048, 1024], P(None, 'kv'), may hold values from -0.125 to 0.125
- q_gain: float32 [128], replicated, may hold values from 0.25 to 1.75
- k_gain: float32 [128], replicated, may hold values from 0.25 to 1.75
- o_proj: bfloat16 [2048, 2048], P('kv'), may hold values from -0.125 to 0.125
- ffn_gain: float32 [2048], replicated, may hold values from 0.25 to 1.75
- w_gate: bfloat16 [2048, 6144], P(None, 'req'), may hold values from -0.125 to 0.125
- w_up: bfloat16 [2048, 6144], P(None, 'req'), may hold values from -0.125 to 0.125
- w_down: bfloat16 [6144, 2048], P('req'), may hold values from -0.078125 to 0.078125
- final_gain: float32 [2048], replicated, may hold values from 0.25 to 1.75
- lm_head: bfloat16 [2048, 151936], P(None, ('req', 'kv')), may hold values from -0.375 to 0.375
Outputs:
- layer_out: bfloat16 [8192, 2048], P(('req', 'kv'))
- max_logit: float32 [72], replicated
Inputs may be any that keep to these rules, and one draw needn't show every extreme that they name: slot_tokens is a permutation of the batch's tokens; each device's 256 consecutive slots take exactly 8 tokens from each device's 256 consecutive batch tokens.
All inputs are finite; a program needn't handle non-finite values. No bound on the sum of `cache_len` on one device may be relied on, other than what follows from the above.
Results may differ from a plain program's by a relative error of at most 0.0085.
The roundings to bfloat16 on the way count: a program that leaves them out, or rounds other values in their place, can miss the bound.
Values may be sent and summed in bfloat16 or wider, within the bound.
No kernel may reach another device: no remote copies, remote signals or barrier semaphores. Data moves between devices by JAX's collectives and lax.ppermute only.
A program may use at most 192 MiB of HBM per device.

v0:
```python
import jax
import jax.numpy as jnp
from jax import lax
from jax.sharding import PartitionSpec as P

EPS = 1e-06
NEG = -1e30


def spread(value, axis, root):
    mine = lax.axis_index(axis) == root
    return lax.psum(jnp.where(mine, value, jnp.zeros_like(value)), axis)


def norm_rows(values, gain_vec):
    wide = values.astype(jnp.float32)
    return wide * lax.rsqrt(jnp.mean(wide * wide, axis=-1, keepdims=True) + EPS) * gain_vec


def rotate(values, places):
    half_dim = values.shape[-1] // 2
    freqs = 1000000.0 ** (-(jnp.arange(half_dim, dtype=jnp.float32) * 2.0 / values.shape[-1]))
    angles = places[:, None] * freqs[None, :]
    cosine = jnp.cos(angles)[:, None, :]
    sine = jnp.sin(angles)[:, None, :]
    first_half = values[..., :half_dim]
    second_half = values[..., half_dim:]
    return jnp.concatenate(
        [first_half * cosine - second_half * sine, second_half * cosine + first_half * sine],
        axis=-1,
    )


def prefill_full(q_heads, key_old, value_old, key_new, value_new, start_at):
    old_len = key_old.shape[0]
    fresh_rows = q_heads.shape[0]
    factor = q_heads.shape[-1] ** (-0.5)
    all_keys = jnp.concatenate([key_old, key_new], axis=0)
    all_values = jnp.concatenate([value_old, value_new], axis=0)
    scores = (
        jnp.einsum("cgd,kd->gck", q_heads, all_keys, preferred_element_type=jnp.float32) * factor
    )
    key_index = jnp.arange(old_len + fresh_rows, dtype=jnp.int32)[None, :]
    row_index = jnp.arange(fresh_rows, dtype=jnp.int32)[:, None]
    allowed = jnp.where(key_index < old_len, key_index < start_at, key_index - old_len <= row_index)
    scores = jnp.where(allowed[None], scores, NEG)
    row_peak = jnp.max(scores, axis=-1, keepdims=True)
    expd = jnp.exp(scores - row_peak)
    weights = (expd / jnp.sum(expd, axis=-1, keepdims=True)).astype(jnp.bfloat16)
    return jnp.einsum(
        "gck,kd->cgd", weights, all_values, preferred_element_type=jnp.float32
    ).astype(jnp.bfloat16)


def decode_attend(q_heads, key_old, value_old, key_self, value_self, lengths):
    factor = q_heads.shape[-1] ** (-0.5)
    past = jnp.einsum("bgd,bld->bgl", q_heads, key_old, preferred_element_type=jnp.float32) * factor
    slot_index = jnp.arange(key_old.shape[1], dtype=jnp.int32)
    past = jnp.where(slot_index[None, None, :] < lengths[:, None, None], past, NEG)
    own_score = (
        jnp.einsum("bgd,bd->bg", q_heads, key_self, preferred_element_type=jnp.float32) * factor
    )
    row_peak = jnp.maximum(jnp.max(past, axis=-1), own_score)
    past_exp = jnp.exp(past - row_peak[..., None])
    own_exp = jnp.exp(own_score - row_peak)
    row_total = jnp.sum(past_exp, axis=-1) + own_exp
    past_w = (past_exp / row_total[..., None]).astype(jnp.bfloat16)
    own_w = (own_exp / row_total).astype(jnp.bfloat16)
    summed = jnp.einsum("bgl,bld->bgd", past_w, value_old, preferred_element_type=jnp.float32)
    summed = (
        summed + own_w.astype(jnp.float32)[..., None] * value_self.astype(jnp.float32)[:, None, :]
    )
    return summed.astype(jnp.bfloat16)


def regroup(rows_in):
    return lax.all_to_all(rows_in, ("req", "kv"), split_axis=0, concat_axis=0, tiled=True)


def shards(
    hidden_in,
    slot_tokens,
    cache_len,
    prefill_start,
    key_cache,
    value_cache,
    key_prefix,
    value_prefix,
    attn_gain,
    q_proj,
    k_proj,
    v_proj,
    q_gain,
    k_gain,
    o_proj,
    ffn_gain,
    w_gate,
    w_up,
    w_down,
    final_gain,
    lm_head,
):
    req_count = lax.axis_size("req")
    kv_count = lax.axis_size("kv")
    devices = req_count * kv_count
    rows_dev = hidden_in.shape[0]
    per_pair = rows_dev // devices
    self_index = lax.axis_index("req") * kv_count + lax.axis_index("kv")
    slot_table = slot_tokens.reshape(devices, rows_dev)
    from_self = slot_table // rows_dev == self_index
    picked = jnp.argsort(jnp.where(from_self, 0, 1).astype(jnp.int32), axis=1, stable=True)[
        :, :per_pair
    ]
    send_rows = (jnp.take_along_axis(slot_table, picked, axis=1) - self_index * rows_dev).reshape(
        -1
    )
    own_sources = lax.dynamic_index_in_dim(slot_table, self_index, 0, keepdims=False) // rows_dev
    marks = (own_sources[:, None] == jnp.arange(devices, dtype=jnp.int32)[None, :]).astype(
        jnp.int32
    )
    ranks = jnp.sum(marks * (jnp.cumsum(marks, axis=0) - 1), axis=1)
    slot_place = own_sources * per_pair + ranks
    arrived = regroup(hidden_in[send_rows])
    owner_rows = arrived[slot_place]
    normed = norm_rows(owner_rows, attn_gain).astype(jnp.bfloat16)
    q_cols = q_proj.shape[1]
    kv_cols = k_proj.shape[1]
    rows_piece = lax.all_gather(normed, "kv", axis=0, tiled=True)
    projected = jnp.concatenate(
        [
            jnp.dot(rows_piece, q_proj, preferred_element_type=jnp.float32),
            jnp.dot(rows_piece, k_proj, preferred_element_type=jnp.float32),
            jnp.dot(rows_piece, v_proj, preferred_element_type=jnp.float32),
        ],
        axis=1,
    )
    tok_req = projected.shape[0]
    head_dim = q_gain.shape[0]
    dec_count = cache_len.shape[0]
    fresh_count = tok_req - dec_count
    q_raw = projected[:, :q_cols].reshape(tok_req, q_cols // head_dim, head_dim)
    k_raw = projected[:, q_cols : q_cols + kv_cols].reshape(tok_req, kv_cols // head_dim, head_dim)
    v_new = (
        projected[:, q_cols + kv_cols :]
        .astype(jnp.bfloat16)
        .reshape(tok_req, kv_cols // head_dim, head_dim)
    )
    places = jnp.concatenate(
        [prefill_start[0] + jnp.arange(fresh_count, dtype=jnp.int32), cache_len]
    ).astype(jnp.float32)
    queries = rotate(norm_rows(q_raw, q_gain), places).astype(jnp.bfloat16)
    keys_new = rotate(norm_rows(k_raw, k_gain), places).astype(jnp.bfloat16)
    kv_local = kv_cols // head_dim
    group_size = q_cols // head_dim // kv_local
    pieces = []
    for head_id in range(kv_local):
        col_lo = head_id * head_dim
        col_hi = col_lo + head_dim
        q_group = queries[:, head_id * group_size : (head_id + 1) * group_size]
        pre_out = prefill_full(
            q_group[:fresh_count],
            key_prefix[0, :, col_lo:col_hi],
            value_prefix[0, :, col_lo:col_hi],
            keys_new[:fresh_count, head_id],
            v_new[:fresh_count, head_id],
            prefill_start[0],
        )
        dec_out = decode_attend(
            q_group[fresh_count:],
            key_cache[:, :, col_lo:col_hi],
            value_cache[:, :, col_lo:col_hi],
            keys_new[fresh_count:, head_id],
            v_new[fresh_count:, head_id],
            cache_len,
        )
        pieces.append(jnp.concatenate([pre_out, dec_out], axis=0))
    attended = jnp.concatenate(pieces, axis=1).reshape(tok_req, q_cols)
    attn_part = lax.psum_scatter(
        jnp.dot(attended, o_proj, preferred_element_type=jnp.float32),
        "kv",
        scatter_dimension=0,
        tiled=True,
    )
    resid = (owner_rows.astype(jnp.float32) + attn_part).astype(jnp.bfloat16)
    ffn_in = norm_rows(resid, ffn_gain).astype(jnp.bfloat16)
    rows_piece = lax.all_gather(ffn_in, "req", axis=0, tiled=True)
    gate_part = jnp.dot(rows_piece, w_gate, preferred_element_type=jnp.float32)
    up_part = jnp.dot(rows_piece, w_up, preferred_element_type=jnp.float32)
    hidden_act = (jax.nn.silu(gate_part) * up_part).astype(jnp.bfloat16)
    ffn_part = lax.psum_scatter(
        jnp.dot(hidden_act, w_down, preferred_element_type=jnp.float32),
        "req",
        scatter_dimension=0,
        tiled=True,
    )
    out_rows = (resid.astype(jnp.float32) + ffn_part).astype(jnp.bfloat16)
    going_back = jnp.zeros_like(out_rows).at[slot_place].set(out_rows)
    returned = regroup(going_back)
    layer_out = jnp.zeros_like(hidden_in).at[send_rows].set(returned)
    tail_rows = norm_rows(out_rows[rows_dev - dec_count - 1 :], final_gain).astype(jnp.bfloat16)
    tail_rows = spread(tail_rows, "kv", kv_count - 1)
    local_peaks = jnp.max(
        jnp.dot(
            lax.all_gather(tail_rows, "req", axis=0, tiled=True),
            lm_head,
            preferred_element_type=jnp.float32,
        ),
        axis=1,
    )
    max_logit = lax.pmax(local_peaks, ("req", "kv"))
    return (layer_out, max_logit)


def solution(mesh):
    placed = (
        P(("req", "kv"), None),
        P(),
        P("req"),
        P("req"),
        P("req", None, "kv"),
        P("req", None, "kv"),
        P("req", None, "kv"),
        P("req", None, "kv"),
        P(),
        P(None, "kv"),
        P(None, "kv"),
        P(None, "kv"),
        P(),
        P(),
        P("kv", None),
        P(),
        P(None, "req"),
        P(None, "req"),
        P("req", None),
        P(),
        P(None, ("req", "kv")),
    )
    return jax.shard_map(
        shards, mesh=mesh, in_specs=placed, out_specs=(P(("req", "kv"), None), P()), check_vma=False
    )
```

profile of v0, /device:TPU:0, one launch (start us, length us, event | category | flops | bytes accessed | tf_op | source)
XLA Modules:
  0.0 856.1 jit_solution(9354852192376584198)
XLA Ops:
  9.4 4.4 sort.19.cloned.1.call-done
  17.8 4.7 gather_fusion
  22.5 7.4 all-to-all-start
  31.5 24.6 %all-to-all-done = bf16[32,8,2048]{2,1,0:T(8,128)(2,1)} async-done(((bf16[32,8,2048]{2,1,0:T(8,128)(2,1)}), bf16[32,8,2048]{2,1,0:T(8,128)(2,1)}, u32[]{:S(2)}, u32[]{:S(2)}) %all-to-all-start) | async-done | bytes 1048608 | tf_op jit(solution)/shard_map/all_to_all | solution.py:77
  56.1 4.7 gather_fusion.1
  73.2 4.0 fusion.8
  77.2 21.3 %all-gather.4.cloned.1.call-done = bf16[1024,2048]{1,0:T(8,128)(2,1)} async-done(((bf16[256,2048]{1,0:T(8,128)(2,1)}), bf16[1024,2048]{1,0:T(8,128)(2,1)}) %all-gather.4.cloned.1.call-update) | async-done | bytes 4194320 | tf_op jit(solution)/shard_map/all_gather | solution.py:128
  98.5 4.8 multiply_reduce_fusion.1
  145.5 15.6 %fusion.131 = (f32[2,1016]{1,0:T(2,128)S(1)}, f32[2,1016,3064]{2,1,0:T(8,128)}) fusion(pred[1016,3064]{1,0:T(8,128)(4,1)} %fusion.8, bf16[1016,128]{1,0:T(8,128)(2,1)} %get-tuple-element.17, bf16[2048,128]{1,0:T(8,128)(2,1)} %get-tuple-element.15, bf16[1024,4,64]{2,0,1:T(8,128)(2,1)} %copy-done.4, bf16[1024,4,64]{2,0,1:T(8,128)(2,1)} %copy-done.5), kind=kOutput, calls=%fused_computation.221 | convolution fusion | flops 1621384704 | bytes 29858304 | tf_op jit(solution)/shard_map/sub | solution.py:48
  161.1 15.7 %fusion.137 = (f32[2,1016]{1,0:T(2,128)S(1)}, f32[2,1016,3064]{2,1,0:T(8,128)}) fusion(pred[1016,3064]{1,0:T(8,128)(4,1)} %fusion.8, bf16[1016,128]{1,0:T(8,128)(2,1)S(1)} %copy-done.8, bf16[2048,128]{1,0:T(8,128)(2,1)} %get-tuple-element.14, bf16[1024,4,64]{2,0,1:T(8,128)(2,1)} %copy-done.4, bf16[1024,4,64]{2,0,1:T(8,128)(2,1)} %copy-done.5), kind=kOutput, calls=%fused_computation.223 | convolution fusion | flops 1621384704 | bytes 29858304 | tf_op jit(solution)/shard_map/sub | solution.py:48
  176.8 12.6 %fusion.50 = bf16[1016,2,128]{2,0,1:T(8,128)(2,1)} fusion(f32[2,1016,3064]{2,1,0:T(8,128)} %get-tuple-element.37, f32[2,1016]{1,0:T(2,128)S(1)} %get-tuple-element.36, bf16[1016,128]{1,0:T(8,128)(2,1)} %bitcast.164, bf16[2048,128]{1,0:T(8,128)(2,1)} %get-tuple-element.13), kind=kOutput, calls=%fused_computation.65 | convolution fusion | flops 1608149248 | bytes 26216896 | tf_op jit(solution)/shard_map/gck,kd->cgd/dot_general | solution.py:50
  189.5 12.5 %fusion.49 = bf16[1016,2,128]{2,0,1:T(8,128)(2,1)} fusion(f32[2,1016,3064]{2,1,0:T(8,128)} %get-tuple-element.41, f32[2,1016]{1,0:T(2,128)S(1)} %get-tuple-element.40, bf16[1016,128]{1,0:T(8,128)(2,1)S(1)} %bitcast.163, bf16[2048,128]{1,0:T(8,128)(2,1)} %get-tuple-element.12), kind=kOutput, calls=%fused_computation.64 | convolution fusion | flops 1608149248 | bytes 26216896 | tf_op jit(solution)/shard_map/gck,kd->cgd/dot_general | solution.py:50
  206.9 7.5 fusion.142
  214.5 71.8 %reduce-scatter.3.cloned.1.call-done = f32[256,2048]{1,0:T(8,128)} async-done(((f32[1024,2048]{1,0:T(8,128)}), f32[256,2048]{1,0:T(8,128)}) %reduce-scatter.3.cloned.1.call-update) | async-done | bytes 2097168 | tf_op jit(solution)/shard_map/reduce_scatter | solution.py:178
  290.9 125.0 %all-gather.6.cloned.1.call-done = bf16[2048,2048]{1,0:T(8,128)(2,1)} async-done(((bf16[256,2048]{1,0:T(8,128)(2,1)}), bf16[2048,2048]{1,0:T(8,128)(2,1)}) %all-gather.6.cloned.1.call-update) | async-done | bytes 8388624 | tf_op jit(solution)/shard_map/all_gather | solution.py:186
  415.9 11.7 %fusion.143 = f32[2048,768]{1,0:T(8,128)} fusion(bf16[2048,2048]{1,0:T(8,128)(2,1)} %all-gather.6.cloned.1.call-done, bf16[2048,768]{1,0:T(8,128)(2,1)} %param.37), kind=kOutput, calls=%fused_computation.225 | convolution fusion | flops 6442450944 | bytes 17825792 | tf_op jit(solution)/shard_map/dot_general | solution.py:187
  427.7 22.5 %fusion.21 = f32[2048,2048]{1,0:T(8,128)} fusion(bf16[768,2048]{1,0:T(8,128)(2,1)S(1)} %copy-done, f32[2048,768]{1,0:T(8,128)} %fusion.143, bf16[2048,2048]{1,0:T(8,128)(2,1)} %all-gather.6.cloned.1.call-done, bf16[2048,768]{1,0:T(8,128)(2,1)} %param.38), kind=kOutput, calls=%fused_computation.34 | convolution fusion | flops 12894339072 | bytes 37748736 | tf_op jit(solution)/shard_map/dot_general | solution.py:191
  450.2 280.3 %reduce-scatter.5.cloned.1.call-done = f32[256,2048]{1,0:T(8,128)} async-done(((f32[2048,2048]{1,0:T(8,128)}), f32[256,2048]{1,0:T(8,128)}) %reduce-scatter.5.cloned.1.call-update) | async-done | bytes 2097168 | tf_op jit(solution)/shard_map/reduce_scatter | solution.py:190
  733.6 3.9 scatter_custom_fusion
  743.2 14.3 %psum.7 = bf16[9,2048]{1,0:T(8,128)(2,1)S(1)} all-reduce(bf16[9,2048]{1,0:T(8,128)(2,1)S(1)} %fusion.73), channel_id=1, replica_groups=mesh['req'=8,'kv'=4] {'kv'}, use_global_device_ids=true, to_apply=%region_21.22 | all-reduce | flops 18432 | bytes 73728 | tf_op jit(solution)/shard_map/psum | solution.py:12
  757.5 34.5 %all-gather = bf16[8,9,2048]{2,1,0:T(8,128)(2,1)} all-gather(bf16[1,9,2048]{2,1,0:T(8,128)(2,1)S(1)} %bitcast.162), channel_id=1, replica_groups=mesh['req'=8,'kv'=4] {'req'}, dimensions={0}, use_global_device_ids=true | all-gather | bytes 331776 | tf_op jit(solution)/shard_map/all_gather | solution.py:204
  793.2 12.6 %convolution_reduce_fusion = f32[72]{0:T(128)S(1)} fusion(bf16[72,2048]{1,0:T(8,128)(2,1)S(1)} %reshape.448, bf16[2048,4748]{0,1:T(8,128)(2,1)} %param.41), kind=kOutput, calls=%fused_computation.63 | convolution fusion | flops 1400583936 | bytes 19743008 | tf_op jit(solution)/shard_map/dot_general | solution.py:203
  805.9 39.5 %pmax.7 = f32[72]{0:T(128)} all-reduce(f32[72]{0:T(128)S(1)} %convolution_reduce_fusion), channel_id=1, replica_groups=mesh['req'=8,'kv'=4] {'req','kv'}, use_global_device_ids=true, to_apply=%region_23.24 | all-reduce | flops 72 | bytes 576 | tf_op jit(solution)/shard_map/pmax | solution.py:210
  845.4 3.8 scatter_custom_fusion.1
  (150 shorter events, 80.8 us)
Async XLA Ops:
  7.2 420.5 %copy-start = (bf16[768,2048]{1,0:T(8,128)(2,1)S(1)}, bf16[768,2048]{1,0:T(8,128)(2,1)}, u32[]{:S(2)}) copy-start(bf16[768,2048]{1,0:T(8,128)(2,1)} %param.39) | copy-start | bytes 9437188
  7.2 6.6 sort.19.cloned.1.call-start
  22.5 33.6 %all-to-all-start = ((bf16[32,8,2048]{2,1,0:T(8,128)(2,1)}), bf16[32,8,2048]{2,1,0:T(8,128)(2,1)}, u32[]{:S(2)}, u32[]{:S(2)}) async-start(bf16[32,8,2048]{2,1,0:T(8,128)(2,1)} %bitcast.155), calls=%async_computation | async-start | bytes 2097152 | tf_op jit(solution)/shard_map/all_to_all | solution.py:77
  29.9 68.7 %all-gather.4.cloned.1.call-start = ((), (), s32[]{:S(2)}) async-start(), calls=%async_computation.4 | async-start | bytes 5242880 | tf_op jit(solution)/shard_map/all_gather | solution.py:128
  56.1 6.2 copy-start.15
  60.8 5.1 copy-start.25
  64.9 221.4 %reduce-scatter.3.cloned.1.call-start = ((), (), s32[]{:S(2)}) async-start(), calls=%async_computation.5 | async-start | bytes 10485760 | tf_op jit(solution)/shard_map/reduce_scatter | solution.py:178
  65.1 7.0 copy-start.6
  77.2 28.7 %copy-start.26 = (f32[128]{0:T(128)S(1)}, f32[128]{0:T(128)}, u32[]{:S(2)}) copy-start(f32[128]{0:T(128)} %param.34) | copy-start | bytes 1540
  107.5 3.6 copy-start.27
  107.5 3.6 copy-start.29
  123.2 4.4 copy-start.4
  123.2 4.4 copy-start.5
  129.8 6.5 copy-start.10
  145.4 15.6 %copy-start.8 = (bf16[1016,128]{1,0:T(8,128)(2,1)S(1)}, bf16[1016,128]{1,0:T(8,128)(2,1)}, u32[]{:S(2)}) copy-start(bf16[1016,128]{1,0:T(8,128)(2,1)} %get-tuple-element.16) | copy-start | bytes 780292
  176.8 12.6 %copy-start.7 = (bf16[1016,1,128]{2,0,1:T(8,128)(2,1)S(1)}, bf16[1016,1,128]{2,0,1:T(8,128)(2,1)}, u32[]{:S(2)}) copy-start(bf16[1016,1,128]{2,0,1:T(8,128)(2,1)} %copy.71) | copy-start | bytes 780292
  189.5 12.6 %copy-start.18 = (f32[8,2,128]{2,1,0:T(2,128)S(1)}, f32[8,2,128]{2,1,0:T(2,128)}, u32[]{:S(2)}) copy-start(f32[8,2,128]{2,1,0:T(2,128)} %fusion.13) | copy-start | bytes 24580
  189.5 12.6 %copy-start.21 = (f32[8,2]{0,1:T(2,128)S(1)}, f32[8,2]{0,1:T(2,128)}, u32[]{:S(2)}) copy-start(f32[8,2]{0,1:T(2,128)} %copy.63) | copy-start | bytes 196
  189.5 12.6 %copy-start.22 = (f32[8,2]{0,1:T(2,128)S(1)}, f32[8,2]{0,1:T(2,128)}, u32[]{:S(2)}) copy-start(f32[8,2]{0,1:T(2,128)} %copy.58) | copy-start | bytes 196
  214.4 75.1 %copy-start.16 = (f32[2048]{0:T(1024)S(1)}, f32[2048]{0:T(1024)}, u32[]{:S(2)}) copy-start(f32[2048]{0:T(1024)} %param.36) | copy-start | bytes 24580
  214.5 201.5 %all-gather.6.cloned.1.call-start = ((), (), s32[]{:S(2)}) async-start(), calls=%async_computation.6 | async-start | bytes 9437184 | tf_op jit(solution)/shard_map/all_gather | solution.py:186
  290.8 439.7 %reduce-scatter.5.cloned.1.call-start = ((), (), s32[]{:S(2)}) async-start(), calls=%async_computation.7 | async-start | bytes 18874368 | tf_op jit(solution)/shard_map/reduce_scatter | solution.py:190
  450.2 292.0 %copy-start.17 = (f32[2048]{0:T(1024)S(1)}, f32[2048]{0:T(1024)}, u32[]{:S(2)}) copy-start(f32[2048]{0:T(1024)} %param.40) | copy-start | bytes 24580
  737.5 107.9 %all-to-all-start.1 = ((bf16[32,8,2048]{2,1,0:T(8,128)(2,1)}), bf16[32,8,2048]{2,1,0:T(8,128)(2,1)}, u32[]{:S(2)}, u32[]{:S(2)}) async-start(bf16[32,8,2048]{2,1,0:T(8,128)(2,1)} %bitcast.156), calls=%async_computation.3 | async-start | bytes 2097152 | tf_op jit(solution)/shard_map/all_to_all | solution.py:77
  (13 other events, 23.5 us)
Sparse Core Ops, SparseCore 0:
  10.9 2.5 sort.21.cloned.1.call-done
  65.0 33.4 all-gather.3
  214.6 71.6 reduce-scatter.2
  290.9 124.9 all-gather.5
  450.3 280.1 reduce-scatter.4
  (1 shorter events, 0.0 us)
where the time goes:
time: 862 us; the launch traced here: 856 us
  waiting for transfers between devices  523 us (61%)
  matrix products  135 us (16%)
  blocking collectives  88.4 us (10%)
  local copies, waits for them, and re-layouts  46.7 us (5%)
  other arithmetic  35.9 us (4%)
  between operations  15.4 us (2%)
  starting transfers between devices  11.5 us (1%)
    reduce_scatter x1, waiting for transfers between devices, shards(): lax.psum_scatter(jnp.dot(hidden_act, w_down, preferred_element_type=jnp.f...  280 us
    all_gather x1, waiting for transfers between devices, shards(): rows_piece = lax.all_gather(ffn_in, 'req', axis=0, tiled=True)  125 us
    reduce_scatter x1, waiting for transfers between devices, shards(): lax.psum_scatter(jnp.dot(attended, o_proj, preferred_element_type=jnp.flo...  71.8 us
    pmax x1, blocking collectives, shards(): max_logit = lax.pmax(local_peaks, ('req', 'kv'))  39.5 us
    all_gather x1, blocking collectives, shards(): lax.all_gather(tail_rows, 'req', axis=0, tiled=True)  34.5 us
    sub x2, matrix products, prefill_full(): expd = jnp.exp(scores - row_peak)  31.4 us
    dot_general x2, matrix products, prefill_full(): jnp.einsum('gck,kd->cgd', weights, all_values, preferred_element_type=jnp...  25.2 us
    all_to_all x2, waiting for transfers between devices, regroup(): lax.all_to_all(rows_in, ('req', 'kv'), split_axis=0, concat_axis=0, tiled...  24.6 us
  transfers between devices with their start and end apart: 6, of which 5 were waited for; matrix products, arithmetic and copies ran while one was open for 3% of the time, Pallas kernels for 0%

commit v1 on v0

v1 whole, which is shorter than its diff:
```python
import jax
import jax.numpy as jnp
from jax import lax
from jax.sharding import PartitionSpec as P

EPS = 1e-06
NEG = -1e30
GROUP = 4


def swap(value, axis, bit):
    size = lax.axis_size(axis)
    return lax.ppermute(value, axis, [(i, i ^ bit) for i in range(size)])


def bits_below(size):
    return [1 << i for i in range(size.bit_length() - 1)]


def gather_xor(value, axis, bits):
    held = {0: value}
    for bit in bits:
        held.update({diff ^ bit: swap(block, axis, bit) for diff, block in list(held.items())})
    return held


def zero_after(value):
    first = value[(0,) * value.ndim]
    return (first != first).astype(jnp.int32)


def norm_rows(values, gain_vec):
    wide = values.astype(jnp.float32)
    return wide * lax.rsqrt(jnp.mean(wide * wide, axis=-1, keepdims=True) + EPS) * gain_vec


def angle_tables(places, head_dim):
    half_dim = head_dim // 2
    freqs = 1000000.0 ** (-(jnp.arange(half_dim, dtype=jnp.float32) * 2.0 / head_dim))
    angles = places[:, None] * freqs[None, :]
    return jnp.cos(angles), jnp.sin(angles)


def rotate(values, cosine, sine):
    half_dim = values.shape[-1] // 2
    cosine, sine = cosine[:, None, :], sine[:, None, :]
    first_half = values[..., :half_dim]
    second_half = values[..., half_dim:]
    return jnp.concatenate(
        [first_half * cosine - second_half * sine, second_half * cosine + first_half * sine],
        axis=-1,
    )


def prefill_full(q_heads, key_old, value_old, key_new, value_new, start_at, order):
    old_len = key_old.shape[0]
    fresh_rows = q_heads.shape[0]
    factor = q_heads.shape[-1] ** (-0.5)
    all_keys = jnp.concatenate([key_old, key_new], axis=0)
    all_values = jnp.concatenate([value_old, value_new], axis=0)
    scores = (
        jnp.einsum("cgd,kd->gck", q_heads, all_keys, preferred_element_type=jnp.float32) * factor
    )
    key_index = jnp.arange(old_len + fresh_rows, dtype=jnp.int32)[None, :]
    key_order = jnp.concatenate([jnp.zeros((old_len,), jnp.int32), order])[None, :]
    allowed = jnp.where(key_index < old_len, key_index < start_at, key_order <= order[:, None])
    scores = jnp.where(allowed[None], scores, NEG)
    row_peak = jnp.max(scores, axis=-1, keepdims=True)
    expd = jnp.exp(scores - row_peak)
    weights = (expd / jnp.sum(expd, axis=-1, keepdims=True)).astype(jnp.bfloat16)
    return jnp.einsum(
        "gck,kd->cgd", weights, all_values, preferred_element_type=jnp.float32
    ).astype(jnp.bfloat16)


def decode_attend(q_heads, key_old, value_old, key_self, value_self, lengths):
    factor = q_heads.shape[-1] ** (-0.5)
    past = jnp.einsum("bgd,bld->bgl", q_heads, key_old, preferred_element_type=jnp.float32) * factor
    slot_index = jnp.arange(key_old.shape[1], dtype=jnp.int32)
    past = jnp.where(slot_index[None, None, :] < lengths[:, None, None], past, NEG)
    own_score = (
        jnp.einsum("bgd,bd->bg", q_heads, key_self, preferred_element_type=jnp.float32) * factor
    )
    row_peak = jnp.maximum(jnp.max(past, axis=-1), own_score)
    past_exp = jnp.exp(past - row_peak[..., None])
    own_exp = jnp.exp(own_score - row_peak)
    row_total = jnp.sum(past_exp, axis=-1) + own_exp
    past_w = (past_exp / row_total[..., None]).astype(jnp.bfloat16)
    own_w = (own_exp / row_total).astype(jnp.bfloat16)
    summed = jnp.einsum("bgl,bld->bgd", past_w, value_old, preferred_element_type=jnp.float32)
    summed = (
        summed + own_w.astype(jnp.float32)[..., None] * value_self.astype(jnp.float32)[:, None, :]
    )
    return summed.astype(jnp.bfloat16)


def regroup(rows_in):
    return lax.all_to_all(rows_in, ("req", "kv"), split_axis=0, concat_axis=0, tiled=True)


def matmul(left, right):
    return jnp.dot(left, right, preferred_element_type=jnp.float32)


def routes(slot_tokens, self_index, devices, rows_dev):
    per_pair = rows_dev // devices
    slot_table = slot_tokens.reshape(devices, rows_dev)
    source = slot_table // rows_dev
    places = jnp.arange(rows_dev, dtype=jnp.int32)
    before = (places[:, None] < places[None, :]).astype(jnp.bfloat16)
    from_self = source == self_index
    rank = matmul(from_self.astype(jnp.bfloat16), before).astype(jnp.int32)
    local = slot_table - self_index * rows_dev
    ranked = jnp.where(from_self, rank, -1)[:, None, :] == jnp.arange(per_pair, dtype=jnp.int32)[None, :, None]
    send_rows = jnp.sum(jnp.where(ranked, local[:, None, :], 0), axis=2).reshape(-1)
    send_hot = (send_rows[:, None] == places[None, :]).astype(jnp.bfloat16)
    own = lax.dynamic_index_in_dim(source, self_index, 0, keepdims=False)
    earlier = (own[:, None] == own[None, :]) & (places[:, None] > places[None, :])
    own_rank = jnp.sum(earlier.astype(jnp.int32), axis=1)
    slot_hot = ((own * per_pair + own_rank)[:, None] == places[None, :]).astype(jnp.bfloat16)
    return send_hot, slot_hot


def pick(hot, rows, transposed=False):
    if transposed:
        return lax.dot_general(
            hot, rows, (((0,), (0,)), ((), ())), preferred_element_type=jnp.float32
        ).astype(rows.dtype)
    return matmul(hot, rows).astype(rows.dtype)


def feed_forward(rows, weights):
    total = None
    for w_gate, w_up, w_down in weights:
        gate = matmul(rows, w_gate)
        up = matmul(rows, w_up)
        hidden_act = (jax.nn.silu(gate) * up).astype(jnp.bfloat16)
        part = matmul(hidden_act, w_down)
        total = part if total is None else total + part
    return total


def shards(
    hidden_in,
    slot_tokens,
    cache_len,
    prefill_start,
    key_cache,
    value_cache,
    key_prefix,
    value_prefix,
    attn_gain,
    q_proj,
    k_proj,
    v_proj,
    q_gain,
    k_gain,
    o_proj,
    ffn_gain,
    w_gate,
    w_up,
    w_down,
    final_gain,
    lm_head,
):
    req_count = lax.axis_size("req")
    kv_count = lax.axis_size("kv")
    devices = req_count * kv_count
    rows_dev, width = hidden_in.shape
    kv_index = lax.axis_index("kv")
    self_index = lax.axis_index("req") * kv_count + kv_index
    kv_bits = bits_below(kv_count)
    near_bits = [bit for bit in bits_below(req_count) if bit < GROUP]
    far_bits = [bit for bit in bits_below(req_count) if bit >= GROUP]

    send_hot, slot_hot = routes(slot_tokens, self_index, devices, rows_dev)
    arrived = regroup(pick(send_hot, hidden_in))
    owner_rows = pick(slot_hot, arrived)

    turn = kv_index + zero_after(arrived)
    share = width // kv_count
    down_share = w_down.shape[0] // kv_count
    gate_up_share = jnp.concatenate(
        [
            lax.dynamic_slice_in_dim(w_gate, turn * share, share, 0),
            lax.dynamic_slice_in_dim(w_up, turn * share, share, 0),
        ],
        axis=1,
    )
    down_part = lax.dynamic_slice_in_dim(w_down, turn * down_share, down_share, 0)
    far_gate_up = gather_xor(gate_up_share, "req", far_bits)
    far_down = gather_xor(down_part, "req", far_bits)

    blocks = gather_xor(owner_rows, "kv", kv_bits[::-1])
    head_dim = q_gain.shape[0]
    dec_count = cache_len.shape[0]
    tok_req = rows_dev * kv_count
    fresh_count = tok_req - dec_count
    q_cols = q_proj.shape[1]
    kv_cols = k_proj.shape[1]
    places = jnp.concatenate(
        [prefill_start[0] + jnp.arange(fresh_count, dtype=jnp.int32), cache_len]
    ).astype(jnp.float32)
    cosines, sines = angle_tables(places, head_dim)
    q_blocks, k_blocks, v_blocks, orders = [], [], [], []
    for diff in range(kv_count):
        block_at = (kv_index ^ diff) * rows_dev
        cosine = lax.dynamic_slice_in_dim(cosines, block_at, rows_dev, 0)
        sine = lax.dynamic_slice_in_dim(sines, block_at, rows_dev, 0)
        normed = norm_rows(blocks[diff], attn_gain).astype(jnp.bfloat16)
        q_raw = matmul(normed, q_proj).reshape(rows_dev, q_cols // head_dim, head_dim)
        k_raw = matmul(normed, k_proj).reshape(rows_dev, kv_cols // head_dim, head_dim)
        v_blocks.append(
            matmul(normed, v_proj)
            .astype(jnp.bfloat16)
            .reshape(rows_dev, kv_cols // head_dim, head_dim)
        )
        q_blocks.append(rotate(norm_rows(q_raw, q_gain), cosine, sine).astype(jnp.bfloat16))
        k_blocks.append(rotate(norm_rows(k_raw, k_gain), cosine, sine).astype(jnp.bfloat16))
        orders.append(block_at + jnp.arange(rows_dev, dtype=jnp.int32))
    queries = jnp.concatenate(q_blocks, axis=0)
    keys_new = jnp.concatenate(k_blocks, axis=0)
    v_new = jnp.concatenate(v_blocks, axis=0)
    order = jnp.concatenate(orders)

    o_whole = lax.all_gather(
        lax.dynamic_slice_in_dim(o_proj, zero_after(blocks[kv_count - 1]), o_proj.shape[0], 0),
        "kv",
        axis=0,
        tiled=True,
    )
    ffn_weights = [(w_gate, w_up, w_down)]
    for diff in far_gate_up:
        if diff:
            whole = lax.all_gather(far_gate_up[diff], "kv", axis=0, tiled=True)
            cut = w_gate.shape[1]
            ffn_weights.append(
                (
                    whole[:, :cut],
                    whole[:, cut:],
                    lax.all_gather(far_down[diff], "kv", axis=0, tiled=True),
                )
            )

    kv_local = kv_cols // head_dim
    group_size = q_cols // head_dim // kv_local
    last_block = (kv_index ^ (kv_count - 1)) * rows_dev
    dec_at = last_block + rows_dev - dec_count
    pieces = []
    for head_id in range(kv_local):
        col_lo = head_id * head_dim
        col_hi = col_lo + head_dim
        q_group = queries[:, head_id * group_size : (head_id + 1) * group_size]
        pre_out = prefill_full(
            q_group,
            key_prefix[0, :, col_lo:col_hi],
            value_prefix[0, :, col_lo:col_hi],
            keys_new[:, head_id],
            v_new[:, head_id],
            prefill_start[0],
            order,
        )
        dec_out = decode_attend(
            lax.dynamic_slice_in_dim(q_group, dec_at, dec_count, 0),
            key_cache[:, :, col_lo:col_hi],
            value_cache[:, :, col_lo:col_hi],
            lax.dynamic_slice_in_dim(keys_new[:, head_id], dec_at, dec_count, 0),
            lax.dynamic_slice_in_dim(v_new[:, head_id], dec_at, dec_count, 0),
            cache_len,
        )
        pieces.append(lax.dynamic_update_slice_in_dim(pre_out, dec_out, dec_at, 0))
    attended = jnp.concatenate(pieces, axis=1).reshape(tok_req, q_cols)

    own_heads = jnp.zeros((rows_dev, q_cols * kv_count), jnp.bfloat16)
    for diff in range(kv_count):
        block = attended[diff * rows_dev : (diff + 1) * rows_dev]
        if diff:
            block = swap(block, "kv", diff)
        own_heads = lax.dynamic_update_slice_in_dim(own_heads, block, (kv_index ^ diff) * q_cols, 1)
    resid = (owner_rows.astype(jnp.float32) + matmul(own_heads, o_whole)).astype(jnp.bfloat16)
    ffn_in = norm_rows(resid, ffn_gain).astype(jnp.bfloat16)

    tail_count = dec_count + 1
    tail_raw = jnp.zeros((tail_count, width), jnp.bfloat16)
    for diff in range(kv_count):
        is_last = (kv_index ^ diff) == kv_count - 1
        tail_raw = jnp.where(is_last, blocks[diff][rows_dev - tail_count :], tail_raw)
    tail_share = jnp.concatenate(
        [
            lax.dynamic_slice_in_dim(attended, dec_at - 1, tail_count, 0),
            lax.dynamic_slice_in_dim(tail_raw, kv_index * share, share, 1),
        ],
        axis=1,
    )
    tails = lax.all_gather(tail_share, ("req", "kv"), axis=0, tiled=True).reshape(
        req_count, kv_count, tail_count, -1
    )
    tails = tails.transpose(0, 2, 1, 3)
    score_rows = req_count * tail_count
    tail_heads = tails[..., :q_cols].reshape(score_rows, -1)
    tail_rows = tails[..., q_cols:].reshape(score_rows, -1)
    tail_resid = (tail_rows.astype(jnp.float32) + matmul(tail_heads, o_whole)).astype(jnp.bfloat16)
    tail_in = norm_rows(tail_resid, ffn_gain).astype(jnp.bfloat16)
    tail_part = feed_forward(tail_in, ffn_weights)
    tail_sent = tail_part.astype(jnp.bfloat16)
    for diff in range(1, GROUP):
        tail_part = tail_part + swap(tail_sent, "req", diff).astype(jnp.float32)
    tail_out = (tail_resid.astype(jnp.float32) + tail_part).astype(jnp.bfloat16)
    tail_normed = norm_rows(tail_out, final_gain).astype(jnp.bfloat16)
    peaks = jnp.max(matmul(tail_normed, lm_head), axis=1)[None, :]
    for axis, bits in (("kv", kv_bits), ("req", bits_below(req_count))):
        for bit in bits:
            peaks = jnp.maximum(peaks, swap(peaks, axis, bit))

    near = gather_xor(ffn_in, "req", near_bits)
    ffn_part = feed_forward(near[0], ffn_weights)
    for diff in range(1, GROUP):
        part = feed_forward(near[diff], ffn_weights).astype(jnp.bfloat16)
        ffn_part = ffn_part + swap(part, "req", diff).astype(jnp.float32)
    out_rows = (resid.astype(jnp.float32) + ffn_part).astype(jnp.bfloat16)
    returned = regroup(pick(slot_hot, out_rows, transposed=True))
    layer_out = pick(send_hot, returned, transposed=True)
    return (layer_out, peaks[0])


def solution(mesh):
    placed = (
        P(("req", "kv"), None),
        P(),
        P("req"),
        P("req"),
        P("req", None, "kv"),
        P("req", None, "kv"),
        P("req", None, "kv"),
        P("req", None, "kv"),
        P(),
        P(None, "kv"),
        P(None, "kv"),
        P(None, "kv"),
        P(),
        P(),
        P("kv", None),
        P(),
        P(None, "req"),
        P(None, "req"),
        P("req", None),
        P(),
        P(None, ("req", "kv")),
    )
    return jax.shard_map(
        shards, mesh=mesh, in_specs=placed, out_specs=(P(("req", "kv"), None), P()), check_vma=False
    )
```

time: 862 us -> 582 us (0.68)
  waiting for transfers between devices: 523 us -> 131 us
  matrix products: 135 us -> 232 us
  starting transfers between devices: 11.5 us -> 22.6 us
  blocking collectives: 88.4 us -> 77.4 us
  local copies, waits for them, and re-layouts: 46.7 us -> 56.5 us
    reduce_scatter x2 -> x0, waiting for transfers between devices: 352 us -> none  [the longest x1 280 us: shards(): lax.psum_scatter(jnp.dot(hidden_act, w_down, preferred_element_type=jnp.f...]
    all_gather x2 -> x3, waiting for transfers between devices: 146 us -> 0.01 us  [the longest x1 0.01 us: shards(): lax.all_gather(lax.dynamic_slice_in_dim(o_proj, zero_after(blocks[kv_coun...]
    ppermute x0 -> x22, waiting for transfers between devices: none -> 130 us  [swap(): return lax.ppermute(value, axis, [(i, i ^ bit) for i in range(size)])]
    dot_general x7 -> x40, matrix products: 64.3 us -> 163 us  [the longest x38 154 us: matmul(): return jnp.dot(left, right, preferred_element_type=jnp.float32)]
    pmax x1 -> x0, blocking collectives: 39.5 us -> none  [shards(): max_logit = lax.pmax(local_peaks, ('req', 'kv'))]
    all_to_all x0 -> x1, blocking collectives: none -> 33.3 us  [regroup(): lax.all_to_all(rows_in, ('req', 'kv'), split_axis=0, concat_axis=0, tiled...]
    all_to_all x2 -> x1, waiting for transfers between devices: 24.6 us -> 0.01 us  [regroup(): lax.all_to_all(rows_in, ('req', 'kv'), split_axis=0, concat_axis=0, tiled...]
    ppermute x0 -> x22, starting transfers between devices: none -> 18.9 us  [swap(): return lax.ppermute(value, axis, [(i, i ^ bit) for i in range(size)])]
  transfers between devices with their start and end apart: 6 -> 26, of which waited for: 5 -> 13; matrix products, arithmetic and copies ran while one was open for 3% -> 56% of each run, Pallas kernels for 0% -> 0%
where the time goes in v1:
time: 582 us; the launch traced here: 576 us
  matrix products  232 us (40%)
  waiting for transfers between devices  131 us (23%)
  blocking collectives  77.4 us (13%)
  local copies, waits for them, and re-layouts  56.5 us (10%)
  other arithmetic  38.9 us (7%)
  starting transfers between devices  22.6 us (4%)
  between operations  17 us (3%)
    dot_general x38, matrix products, matmul(): return jnp.dot(left, right, preferred_element_type=jnp.float32)  154 us
    ppermute x22, waiting for transfers between devices, swap(): return lax.ppermute(value, axis, [(i, i ^ bit) for i in range(size)])  130 us
    all_gather x1, blocking collectives, shards(): lax.all_gather(tail_share, ('req', 'kv'), axis=0, tiled=True)  44 us
    sub x2, matrix products, prefill_full(): expd = jnp.exp(scores - row_peak)  33.6 us
    all_to_all x1, blocking collectives, regroup(): lax.all_to_all(rows_in, ('req', 'kv'), split_axis=0, concat_axis=0, tiled...  33.3 us
    dot_general x2, matrix products, prefill_full(): jnp.einsum('gck,kd->cgd', weights, all_values, preferred_element_type=jnp...  22.1 us
    ppermute x22, starting transfers between devices, swap(): return lax.ppermute(value, axis, [(i, i ^ bit) for i in range(size)])  18.9 us
    reduce_sum x8, other arithmetic, norm_rows(): jnp.mean(wide * wide, axis=-1, keepdims=True) + EPS  12.5 us
  transfers between devices with their start and end apart: 26, of which 13 were waited for; matrix products, arithmetic and copies ran while one was open for 56% of the time, Pallas kernels for 0%

profile of v1, /device:TPU:0, one launch (start us, length us, event | category | flops | bytes accessed | tf_op | source)
XLA Modules:
  0.0 575.6 jit_solution(8026025956311205400)
XLA Ops:
  11.5 33.3 %all_to_all.24 = bf16[32,8,2048]{2,1,0:T(8,128)(2,1)S(1)} all-to-all(bf16[32,8,2048]{2,1,0:T(8,128)(2,1)S(1)} %fusion.32), channel_id=1, replica_groups=mesh['req'=8,'kv'=4] {'req','kv'}, dimensions={0} | all-to-all | bytes 2097152 | tf_op jit(solution)/shard_map/all_to_all | solution.py:98
  50.1 69.6 %collective-permute-done.6 = bf16[512,1536]{1,0:T(8,128)(2,1)} collective-permute-done((bf16[512,1536]{1,0:T(8,128)(2,1)S(1)}, bf16[512,1536]{1,0:T(8,128)(2,1)}, u32[]{:S(2)}, u32[]{:S(2)}) %collective-permute-start.6) | collective-permute-done | bytes 1572896 | tf_op jit(solution)/shard_map/ppermute | solution.py:13
  132.5 4.9 compare_select_fusion
  158.4 24.7 %collective-permute-done.7 = bf16[192,2048]{1,0:T(8,128)(2,1)} collective-permute-done((bf16[192,2048]{1,0:T(8,128)(2,1)}, bf16[192,2048]{1,0:T(8,128)(2,1)}, u32[]{:S(2)}, u32[]{:S(2)}) %collective-permute-start.7) | collective-permute-done | bytes 786464 | tf_op jit(solution)/shard_map/ppermute | solution.py:13
  271.1 16.7 %fusion.249 = (f32[2,1024]{1,0:T(2,128)S(1)}, f32[2,1024,3072]{1,2,0:T(8,128)}) fusion(pred[1024,3072]{0,1:T(8,128)(4,1)} %compare_select_fusion, bf16[1024,128]{1,0:T(8,128)(2,1)S(1)} %copy-done.22, bf16[2048,128]{1,0:T(8,128)(2,1)} %get-tuple-element.12, bf16[1024,4,128]{2,0,1:T(8,128)(2,1)} %copy-done.6), kind=kOutput, calls=%fused_computation.392 | convolution fusion | flops 1637354496 | bytes 29630464 | tf_op jit(solution)/shard_map/sub | solution.py:69
  287.8 11.1 %fusion.87 = bf16[1024,2,128]{0,2,1:T(8,128)(2,1)} fusion(f32[2,1024,3072]{1,2,0:T(8,128)} %get-tuple-element.79, f32[2,1024]{1,0:T(2,128)S(1)} %get-tuple-element.78, bf16[1024,128]{0,1:T(8,128)(2,1)} %get-tuple-element.26, bf16[2048,128]{0,1:T(8,128)(2,1)} %bitcast.232), kind=kOutput, calls=%fused_computation.118 | convolution fusion | flops 1625030656 | bytes 26484736 | tf_op jit(solution)/shard_map/gck,kd->cgd/dot_general | solution.py:71
  300.6 16.9 %fusion.243 = (f32[2,1024]{1,0:T(2,128)S(1)}, f32[2,1024,3072]{1,2,0:T(8,128)}) fusion(pred[1024,3072]{0,1:T(8,128)(4,1)} %compare_select_fusion, bf16[1024,128]{1,0:T(8,128)(2,1)S(1)} %copy-done.21, bf16[2048,128]{1,0:T(8,128)(2,1)} %get-tuple-element.13, bf16[1024,4,128]{2,0,1:T(8,128)(2,1)} %copy-done.6), kind=kOutput, calls=%fused_computation.390 | convolution fusion | flops 1637354496 | bytes 29630464 | tf_op jit(solution)/shard_map/sub | solution.py:69
  317.5 11.0 %fusion.86 = bf16[1024,2,128]{0,2,1:T(8,128)(2,1)} fusion(f32[2,1024,3072]{1,2,0:T(8,128)} %get-tuple-element.75, f32[2,1024]{1,0:T(2,128)S(1)} %get-tuple-element.74, bf16[1024,128]{0,1:T(8,128)(2,1)} %get-tuple-element.25, bf16[2048,128]{0,1:T(8,128)(2,1)} %bitcast.231), kind=kOutput, calls=%fused_computation.117 | convolution fusion | flops 1625030656 | bytes 26484736 | tf_op jit(solution)/shard_map/gck,kd->cgd/dot_general | solution.py:71
  335.7 44.0 %all-gather = bf16[32,9,1024]{2,1,0:T(8,128)(2,1)S(1)} all-gather(bf16[1,9,1024]{2,1,0:T(8,128)(2,1)S(1)} %maximum_bitcast_fusion.18), channel_id=1, replica_groups=mesh['req'=8,'kv'=4] {'req','kv'}, dimensions={0}, use_global_device_ids=true | all-gather | bytes 608256 | tf_op jit(solution)/shard_map/all_gather | solution.py:295
  394.8 6.5 %fusion.60 = (f32[256]{0:T(256)S(1)}, bf16[256,2048]{1,0:T(8,128)(2,1)S(1)}) fusion(bf16[256,2048]{0,1:T(8,128)(2,1)} %constant_dynamic-update-slice_fusion, bf16[2048,2048]{1,0:T(8,128)(2,1)} %all-gather.5.cloned.1.call-done, bf16[256,2048]{1,0:T(8,128)(2,1)} %get-tuple-element.65), kind=kOutput, calls=%fused_computation.79 | convolution fusion | flops 2150629120 | bytes 11535360 | tf_op jit(solution)/shard_map/dot_general | solution.py:102
  410.8 4.1 fusion.264
  414.9 5.9 %fusion.92 = f32[256,2048]{1,0:T(8,128)} fusion(bf16[768,2048]{1,0:T(8,128)(2,1)S(1)} %copy-done, bf16[256,2048]{1,0:T(8,128)(2,1)} %fusion.62, bf16[2048,768]{1,0:T(8,128)(2,1)} %param.38, f32[256,768]{1,0:T(8,128)} %fusion.264), kind=kOutput, calls=%fused_computation.130 | convolution fusion | flops 1611792384 | bytes 10223616 | tf_op jit(solution)/shard_map/dot_general | solution.py:102
  424.2 4.5 collective-permute-done.8
  431.8 6.1 %fusion.111 = f32[256,2048]{1,0:T(8,128)} fusion(bf16[768,2048]{1,0:T(8,128)(2,1)S(1)} %copy-done, f32[256,768]{1,0:T(8,128)} %fusion.265, bf16[256,2048]{1,0:T(8,128)(2,1)} %collective-permute-done.8, bf16[2048,768]{1,0:T(8,128)(2,1)} %param.38), kind=kOutput, calls=%fused_computation.188 | convolution fusion | flops 1611792384 | bytes 10223616 | tf_op jit(solution)/shard_map/dot_general | solution.py:102
  442.0 7.1 %fusion.27 = bf16[256,2048]{1,0:T(8,128)(2,1)} fusion(f32[256,2048]{1,0:T(8,128)} %fusion.111, bf16[768,2048]{1,0:T(8,128)(2,1)} %all-gather.9.cloned.1.call-done, f32[256,768]{1,0:T(8,128)} %fusion.69, bf16[256,2048]{1,0:T(8,128)(2,1)} %collective-permute-done.8, bf16[2048,1536]{1,0:T(8,128)(2,1)} %all-gather.7.cloned.1.call-done), kind=kOutput, calls=%fused_computation.48 | convolution fusion | flops 1612840960 | bytes 11272192 | tf_op jit(solution)/shard_map/dot_general | solution.py:102
  453.4 5.8 %fusion.116 = f32[256,2048]{1,0:T(8,128)} fusion(bf16[768,2048]{1,0:T(8,128)(2,1)S(1)} %copy-done, f32[256,768]{1,0:T(8,128)} %fusion.266, bf16[256,2048]{1,0:T(8,128)(2,1)} %collective-permute-done.10, bf16[2048,768]{1,0:T(8,128)(2,1)} %param.38), kind=kOutput, calls=%fused_computation.189 | convolution fusion | flops 1611792384 | bytes 10223616 | tf_op jit(solution)/shard_map/dot_general | solution.py:102
  463.4 7.2 %fusion.28 = bf16[256,2048]{1,0:T(8,128)(2,1)} fusion(f32[256,2048]{1,0:T(8,128)} %fusion.116, bf16[768,2048]{1,0:T(8,128)(2,1)} %all-gather.9.cloned.1.call-done, f32[256,768]{1,0:T(8,128)} %fusion.67, bf16[256,2048]{1,0:T(8,128)(2,1)} %collective-permute-done.10, bf16[2048,1536]{1,0:T(8,128)(2,1)} %all-gather.7.cloned.1.call-done), kind=kOutput, calls=%fused_computation.49 | convolution fusion | flops 1612840960 | bytes 11272192 | tf_op jit(solution)/shard_map/dot_general | solution.py:102
  483.0 5.8 %fusion.121 = f32[256,2048]{1,0:T(8,128)} fusion(bf16[768,2048]{1,0:T(8,128)(2,1)S(1)} %copy-done, f32[256,768]{1,0:T(8,128)} %fusion.267, bf16[256,2048]{1,0:T(8,128)(2,1)} %collective-permute-done.12, bf16[2048,768]{1,0:T(8,128)(2,1)} %param.38), kind=kOutput, calls=%fused_computation.190 | convolution fusion | flops 1611792384 | bytes 10223616 | tf_op jit(solution)/shard_map/dot_general | solution.py:102
  488.8 7.4 %fusion.29 = bf16[256,2048]{1,0:T(8,128)(2,1)} fusion(f32[256,2048]{1,0:T(8,128)} %fusion.121, bf16[768,2048]{1,0:T(8,128)(2,1)} %all-gather.9.cloned.1.call-done, f32[256,768]{1,0:T(8,128)} %fusion.65, bf16[256,2048]{1,0:T(8,128)(2,1)} %collective-permute-done.12, bf16[2048,1536]{1,0:T(8,128)(2,1)} %all-gather.7.cloned.1.call-done), kind=kOutput, calls=%fused_computation.50 | convolution fusion | flops 1612840960 | bytes 11272192 | tf_op jit(solution)/shard_map/dot_general | solution.py:102
  496.7 5.3 fusion.255
  509.0 4.1 fusion.81
  514.1 9.5 %collective-permute-done.13 = bf16[256,2048]{1,0:T(8,128)(2,1)} collective-permute-done((bf16[256,2048]{1,0:T(8,128)(2,1)}, bf16[256,2048]{1,0:T(8,128)(2,1)}, u32[]{:S(2)}, u32[]{:S(2)}) %collective-permute-start.13) | collective-permute-done | bytes 1048608 | tf_op jit(solution)/shard_map/ppermute | solution.py:13
  523.6 6.8 %fusion.33 = bf16[32,8,2048]{2,1,0:T(8,128)(2,1)} fusion(f32[256,2048]{1,0:T(8,128)} %fusion.92, bf16[768,2048]{1,0:T(8,128)(2,1)} %all-gather.9.cloned.1.call-done, bf16[256,2048]{1,0:T(8,128)(2,1)} %copy-done.7, bf16[256,2048]{1,0:T(8,128)(2,1)} %collective-permute-done.13, bf16[256,2048]{1,0:T(8,128)(2,1)} %collective-permute-done.11, ...), kind=kOutput, calls=%fused_computation.58 | convolution fusion | flops 1080754176 | bytes 12059648 | tf_op jit(solution)/shard_map/dot_general | solution.py:126
  536.4 12.7 %convolution_reduce_fusion = f32[72]{0:T(128)S(1)} fusion(bf16[2048,4748]{0,1:T(8,128)(2,1)} %param.41, bf16[72,2048]{1,0:T(8,128)(2,1)S(1)} %get-tuple-element.3, f32[2048]{0:T(1024)S(1)} %copy-done.31, f32[72]{0:T(128)S(1)} %add_rsqrt_fusion.13), kind=kOutput, calls=%fused_computation.115 | convolution fusion | flops 1401173760 | bytes 19751488 | tf_op jit(solution)/shard_map/dot_general | solution.py:102
  (309 shorter events, 227.6 us)
Async XLA Ops:
  7.2 387.6 %all-gather.5.cloned.1.call-start = ((), (), s32[]{:S(2)}) async-start(), calls=%async_computation.2 | async-start | bytes 10485760 | tf_op jit(solution)/shard_map/all_gather | solution.py:226
  7.9 412.9 %all-gather.7.cloned.1.call-start = ((), (), s32[]{:S(2)}) async-start(), calls=%async_computation.3 | async-start | bytes 7864320 | tf_op jit(solution)/shard_map/all_gather | solution.py:235
  49.3 70.4 %collective-permute-start.6 = (bf16[512,1536]{1,0:T(8,128)(2,1)S(1)}, bf16[512,1536]{1,0:T(8,128)(2,1)}, u32[]{:S(2)}, u32[]{:S(2)}) collective-permute-start(bf16[512,1536]{1,0:T(8,128)(2,1)S(1)} %pad_maximum_fusion.1), channel_id=1, source_target_pairs={{0,16},{4,20},{8,24},{12,28},{16,0},{20,4},{24,8},{28,12},{1,17},{... | collective-permute-start | bytes 4718600 | tf_op jit(solution)/shard_map/ppermute | solution.py:13
  119.7 322.2 %all-gather.9.cloned.1.call-start = ((), (), s32[]{:S(2)}) async-start(), calls=%async_computation.4 | async-start | bytes 3932160 | tf_op jit(solution)/shard_map/all_gather | solution.py:241
  138.9 47.1 %collective-permute-start.1 = (bf16[256,2048]{1,0:T(8,128)(2,1)}, bf16[256,2048]{1,0:T(8,128)(2,1)}, u32[]{:S(2)}, u32[]{:S(2)}) collective-permute-start(bf16[256,2048]{1,0:T(8,128)(2,1)} %get-tuple-element.65), channel_id=1, source_target_pairs={{0,2},{1,3},{2,0},{3,1},{4,6},{5,7},{6,4},{7,5},{8,10},{9,11},{10,... | collective-permute-start | bytes 3145736 | tf_op jit(solution)/shard_map/ppermute | solution.py:13
  140.9 54.3 %collective-permute-start = (bf16[256,2048]{1,0:T(8,128)(2,1)}, bf16[256,2048]{1,0:T(8,128)(2,1)}, u32[]{:S(2)}, u32[]{:S(2)}) collective-permute-start(bf16[256,2048]{1,0:T(8,128)(2,1)} %get-tuple-element.65), channel_id=1, source_target_pairs={{0,1},{1,0},{2,3},{3,2},{4,5},{5,4},{6,7},{7,6},{8,9},{9,8},{10,11... | collective-permute-start | bytes 3145736 | tf_op jit(solution)/shard_map/ppermute | solution.py:13
  146.7 36.4 %collective-permute-start.7 = (bf16[192,2048]{1,0:T(8,128)(2,1)}, bf16[192,2048]{1,0:T(8,128)(2,1)}, u32[]{:S(2)}, u32[]{:S(2)}) collective-permute-start(bf16[192,2048]{1,0:T(8,128)(2,1)} %constant_dynamic-slice_fusion.1), channel_id=1, source_target_pairs={{0,16},{4,20},{8,24},{12,28},{16,0},{20,4},{24,8},{28,12},{1,17},{... | collective-permute-start | bytes 2359304 | tf_op jit(solution)/shard_map/ppermute | solution.py:13
  209.8 15.8 %collective-permute-start.2 = (bf16[256,2048]{1,0:T(8,128)(2,1)}, bf16[256,2048]{1,0:T(8,128)(2,1)}, u32[]{:S(2)}, u32[]{:S(2)}) collective-permute-start(bf16[256,2048]{1,0:T(8,128)(2,1)} %collective-permute-done.1), channel_id=1, source_target_pairs={{0,1},{1,0},{2,3},{3,2},{4,5},{5,4},{6,7},{7,6},{8,9},{9,8},{10,11... | collective-permute-start | bytes 3145736 | tf_op jit(solution)/shard_map/ppermute | solution.py:13
  380.2 5.1 collective-permute-start.3
  380.7 9.4 %collective-permute-start.4 = (bf16[256,512]{0,1:T(8,128)(2,1)}, bf16[256,512]{0,1:T(8,128)(2,1)S(1)}, u32[]{:S(2)}, u32[]{:S(2)}) collective-permute-start(bf16[256,512]{0,1:T(8,128)(2,1)} %bitcast.238), channel_id=1, source_target_pairs={{0,2},{1,3},{2,0},{3,1},{4,6},{5,7},{6,4},{7,5},{8,10},{9,11},{10,... | collective-permute-start | bytes 786440 | tf_op jit(solution)/shard_map/ppermute | solution.py:13
  380.8 13.2 %collective-permute-start.5 = (bf16[256,512]{0,1:T(8,128)(2,1)S(1)}, bf16[256,512]{0,1:T(8,128)(2,1)S(1)}, u32[]{:S(2)}, u32[]{:S(2)}) collective-permute-start(bf16[256,512]{0,1:T(8,128)(2,1)S(1)} %bitcast.237), channel_id=1, source_target_pairs={{0,3},{1,2},{2,1},{3,0},{4,7},{5,6},{6,5},{7,4},{8,11},{9,10},{10,... | collective-permute-start | bytes 786440 | tf_op jit(solution)/shard_map/ppermute | solution.py:13
  402.7 26.0 %collective-permute-start.8 = (bf16[256,2048]{1,0:T(8,128)(2,1)}, bf16[256,2048]{1,0:T(8,128)(2,1)}, u32[]{:S(2)}, u32[]{:S(2)}) collective-permute-start(bf16[256,2048]{1,0:T(8,128)(2,1)} %fusion.62), channel_id=1, source_target_pairs={{0,4},{4,0},{8,12},{12,8},{16,20},{20,16},{24,28},{28,24},{1,5},{5... | collective-permute-start | bytes 3145736 | tf_op jit(solution)/shard_map/ppermute | solution.py:13
  402.7 46.7 %collective-permute-start.10 = (bf16[256,2048]{1,0:T(8,128)(2,1)}, bf16[256,2048]{1,0:T(8,128)(2,1)}, u32[]{:S(2)}, u32[]{:S(2)}) collective-permute-start(bf16[256,2048]{1,0:T(8,128)(2,1)} %fusion.62), channel_id=1, source_target_pairs={{0,8},{4,12},{8,0},{12,4},{16,24},{20,28},{24,16},{28,20},{1,9},{5... | collective-permute-start | bytes 3145736 | tf_op jit(solution)/shard_map/ppermute | solution.py:13
  449.1 64.1 %collective-permute-start.9 = (bf16[256,2048]{1,0:T(8,128)(2,1)}, bf16[256,2048]{1,0:T(8,128)(2,1)}, u32[]{:S(2)}, u32[]{:S(2)}) collective-permute-start(bf16[256,2048]{1,0:T(8,128)(2,1)} %fusion.27), channel_id=1, source_target_pairs={{0,4},{4,0},{8,12},{12,8},{16,20},{20,16},{24,28},{28,24},{1,5},{5... | collective-permute-start | bytes 3145736 | tf_op jit(solution)/shard_map/ppermute | solution.py:13
  449.4 26.4 %collective-permute-start.12 = (bf16[256,2048]{1,0:T(8,128)(2,1)}, bf16[256,2048]{1,0:T(8,128)(2,1)}, u32[]{:S(2)}, u32[]{:S(2)}) collective-permute-start(bf16[256,2048]{1,0:T(8,128)(2,1)} %collective-permute-done.8), channel_id=1, source_target_pairs={{0,8},{4,12},{8,0},{12,4},{16,24},{20,28},{24,16},{28,20},{1,9},{5... | collective-permute-start | bytes 3145736 | tf_op jit(solution)/shard_map/ppermute | solution.py:13
  470.6 43.5 %collective-permute-start.11 = (bf16[256,2048]{1,0:T(8,128)(2,1)}, bf16[256,2048]{1,0:T(8,128)(2,1)}, u32[]{:S(2)}, u32[]{:S(2)}) collective-permute-start(bf16[256,2048]{1,0:T(8,128)(2,1)} %fusion.28), channel_id=1, source_target_pairs={{0,8},{4,12},{8,0},{12,4},{16,24},{20,28},{24,16},{28,20},{1,9},{5... | collective-permute-start | bytes 3145736 | tf_op jit(solution)/shard_map/ppermute | solution.py:13
  496.2 27.4 %collective-permute-start.13 = (bf16[256,2048]{1,0:T(8,128)(2,1)}, bf16[256,2048]{1,0:T(8,128)(2,1)}, u32[]{:S(2)}, u32[]{:S(2)}) collective-permute-start(bf16[256,2048]{1,0:T(8,128)(2,1)} %fusion.29), channel_id=1, source_target_pairs={{0,12},{4,8},{8,4},{12,0},{16,28},{20,24},{24,20},{28,16},{1,13},{... | collective-permute-start | bytes 3145736 | tf_op jit(solution)/shard_map/ppermute | solution.py:13
  502.0 31.9 %collective-permute-start.14 = (bf16[72,2048]{1,0:T(8,128)(2,1)}, bf16[72,2048]{1,0:T(8,128)(2,1)S(1)}, u32[]{:S(2)}, u32[]{:S(2)}) collective-permute-start(bf16[72,2048]{1,0:T(8,128)(2,1)} %get-tuple-element.86), channel_id=1, source_target_pairs={{0,4},{4,0},{8,12},{12,8},{16,20},{20,16},{24,28},{28,24},{1,5},{5... | collective-permute-start | bytes 884744 | tf_op jit(solution)/shard_map/ppermute | solution.py:13
  503.0 30.9 %collective-permute-start.15 = (bf16[72,2048]{1,0:T(8,128)(2,1)}, bf16[72,2048]{1,0:T(8,128)(2,1)}, u32[]{:S(2)}, u32[]{:S(2)}) collective-permute-start(bf16[72,2048]{1,0:T(8,128)(2,1)} %get-tuple-element.86), channel_id=1, source_target_pairs={{0,8},{4,12},{8,0},{12,4},{16,24},{20,28},{24,16},{28,20},{1,9},{5... | collective-permute-start | bytes 884744 | tf_op jit(solution)/shard_map/ppermute | solution.py:13
  513.2 20.8 %collective-permute-start.16 = (bf16[72,2048]{1,0:T(8,128)(2,1)}, bf16[72,2048]{1,0:T(8,128)(2,1)}, u32[]{:S(2)}, u32[]{:S(2)}) collective-permute-start(bf16[72,2048]{1,0:T(8,128)(2,1)} %get-tuple-element.86), channel_id=1, source_target_pairs={{0,12},{4,8},{8,4},{12,0},{16,28},{20,24},{24,20},{28,16},{1,13},{... | collective-permute-start | bytes 884744 | tf_op jit(solution)/shard_map/ppermute | solution.py:13
  530.4 35.5 %all-to-all-start.1 = ((bf16[32,8,2048]{2,1,0:T(8,128)(2,1)}), bf16[32,8,2048]{2,1,0:T(8,128)(2,1)}, u32[]{:S(2)}, u32[]{:S(2)}) async-start(bf16[32,8,2048]{2,1,0:T(8,128)(2,1)} %fusion.33), calls=%async_computation.1 | async-start | bytes 2097152 | tf_op jit(solution)/shard_map/all_to_all | solution.py:98
  550.3 3.5 collective-permute-start.18
  553.9 3.5 collective-permute-start.19
  560.9 4.4 collective-permute-start.21
  (52 other events, 580.0 us)
Sparse Core Ops, SparseCore 0:
  9.6 69.8 all-gather.4
  119.9 67.1 all-gather.6
  188.6 29.0 all-gather.8
